TPU v7x, 32 devices: a whole 2x2x4 slice. The times are simulated.
32 devices in a mesh: fine: 4 (over x, core), coarse: 8 (over z, y).
Axes of the slice: x: 2, y: 2, z: 4, core: 2. Of those that a mesh axis runs over, the one named last changes fastest.
Arguments:
- query_rows: bfloat16 [8192, 768], P(('coarse', 'fine')), may hold values from -6 to 6
- key_rows: bfloat16 [8192, 768], P(('coarse', 'fine')), may hold values from -6 to 6
- value_rows: bfloat16 [8192, 768], P(('coarse', 'fine')), may hold values from -6 to 6
- distance_slope: float32 [12], replicated, may hold values from 0.4 to 1.6
- out_weight: bfloat16 [768, 768], P('coarse'), may hold values from -0.21875 to 0.21875
Outputs:
- mixed: bfloat16 [8192, 768], P(('coarse', 'fine'))
All inputs are finite; a program needn't handle non-finite values.
Results may differ from a plain program's by a relative error of at most 0.0065.
Values may be sent and summed in bfloat16 or wider, within the bound.
A program may use at most 64 MiB of HBM per device.

v0:
```python
import math

import jax
import jax.numpy as jnp
from jax import lax
from jax.sharding import PartitionSpec as P

BLOCK = 128


LOG_TWO = math.log(2.0)


def coarsen(row_data):
    dims_all = row_data.shape
    paired = row_data.reshape(dims_all[:-2] + (dims_all[-2] // 2, 2, dims_all[-1])).astype(
        jnp.float32
    )
    return ((paired[..., 0, :] + paired[..., 1, :]) * 0.5).astype(jnp.bfloat16)


def step_down(q_now):
    if q_now.shape[0] >= 2:
        return coarsen(q_now)
    return q_now


def attend(queries, key_group, value_group, level_gain):
    groups, query_count, width_all = queries.shape
    key_count = key_group.shape[1]
    head_count = level_gain.shape[0]
    head_size = width_all // head_count
    q_heads = queries.reshape(groups, query_count, head_count, head_size)
    k_heads = key_group.reshape(groups, key_count, head_count, head_size)
    v_heads = value_group.reshape(groups, key_count, head_count, head_size)
    scores = (
        jnp.einsum("gqhe,gkhe->ghqk", q_heads, k_heads, preferred_element_type=jnp.float32)
        * (1.0 / math.sqrt(head_size))
        + level_gain[None, :, None, None]
    )
    row_max = jnp.max(scores, axis=3)
    p_weights = jnp.exp(scores - row_max[..., None]).astype(jnp.bfloat16)
    row_sum = jnp.sum(p_weights.astype(jnp.float32), axis=3)
    weighted = jnp.einsum("ghqk,gkhe->gqhe", p_weights, v_heads, preferred_element_type=jnp.float32)
    return (
        jnp.transpose(row_max, (0, 2, 1)).reshape(groups * query_count, head_count),
        weighted.reshape(groups * query_count, width_all),
        jnp.transpose(row_sum, (0, 2, 1)).reshape(groups * query_count, head_count),
    )


def widen(level_stat, factor):
    return tuple((jnp.repeat(member, factor, axis=0) for member in level_stat))


def merge(earlier, latest):
    max_a, numer_a, denom_a = earlier
    max_b, numer_b, denom_b = latest
    row_max = jnp.maximum(max_a, max_b)
    scale_a = jnp.exp(max_a - row_max)
    scale_b = jnp.exp(max_b - row_max)
    row_count, width_all = numer_a.shape
    head_count = row_max.shape[1]
    numer = (
        numer_a.reshape(row_count, head_count, -1) * scale_a[:, :, None]
        + numer_b.reshape(row_count, head_count, -1) * scale_b[:, :, None]
    ).reshape(row_count, width_all)
    denom = denom_a * scale_a + denom_b * scale_b
    return (row_max, numer, denom)


def far_level(combined, q_now, sibling, level_now, distance_slope, tokens):
    level_gain = level_now * LOG_TWO * (1.0 - distance_slope)
    far_stat = attend(q_now[None], sibling[0][None], sibling[1][None], level_gain)
    return merge(combined, widen(far_stat, tokens // q_now.shape[0]))


def on_device(query_rows, key_rows, value_rows, distance_slope, out_weight):
    tokens, width_all = query_rows.shape
    block_len = BLOCK
    pair_len = 2 * block_len
    local_levels = (tokens // block_len).bit_length() - 1
    fine_bits = lax.axis_size("fine").bit_length() - 1
    coarse_bits = lax.axis_size("coarse").bit_length() - 1
    level_now = 0
    combined = attend(
        query_rows.reshape(tokens // pair_len, pair_len, width_all),
        key_rows.reshape(tokens // pair_len, pair_len, width_all),
        value_rows.reshape(tokens // pair_len, pair_len, width_all),
        level_now * LOG_TWO * (1.0 - distance_slope),
    )
    q_now, k_now, v_now = (query_rows, key_rows, value_rows)
    q_now = coarsen(q_now)
    own_pair = coarsen(jnp.stack([k_now, v_now]))
    level_now = local_levels
    group_rows = lax.all_gather(own_pair, "fine", axis=1, tiled=True)
    fine_index = lax.axis_index("fine")
    for bit_no in range(fine_bits):
        partner = fine_index >> bit_no ^ 1
        sibling = lax.dynamic_slice_in_dim(group_rows, partner * block_len, block_len, 1)
        combined = far_level(combined, q_now, sibling, level_now, distance_slope, tokens)
        group_rows = coarsen(group_rows)
        q_now, level_now = (step_down(q_now), level_now + 1)
    group_rows = lax.all_gather(group_rows, "coarse", axis=1, tiled=True)
    coarse_index = lax.axis_index("coarse")
    for bit_no in range(coarse_bits):
        partner = coarse_index >> bit_no ^ 1
        sibling = lax.dynamic_slice_in_dim(group_rows, partner * block_len, block_len, 1)
        combined = far_level(combined, q_now, sibling, level_now, distance_slope, tokens)
        group_rows = coarsen(group_rows)
        q_now, level_now = (step_down(q_now), level_now + 1)
    row_max, numer, denom = combined
    head_count = row_max.shape[1]
    attended = (
        (numer.reshape(tokens, head_count, -1) / denom[:, :, None])
        .reshape(tokens, width_all)
        .astype(jnp.bfloat16)
    )
    projected = jnp.dot(
        attended,
        lax.all_gather(out_weight, "coarse", axis=0, tiled=True),
        preferred_element_type=jnp.float32,
    )
    return projected.astype(jnp.bfloat16)


def solution(mesh):
    return jax.shard_map(
        on_device,
        mesh=mesh,
        in_specs=(
            P(("coarse", "fine"), None),
            P(("coarse", "fine"), None),
            P(("coarse", "fine"), None),
            P(),
            P("coarse", None),
        ),
        out_specs=P(("coarse", "fine"), None),
        check_vma=False,
    )
```

profile of v0, /device:TPU:0, one launch (start us, length us, event | category | flops | bytes accessed | tf_op | source)
XLA Modules:
  0.0 176.5 jit_solution(16658550966408269373)
XLA Ops:
  6.5 1.2 stack.10
  9.0 22.5 %all-gather.8.cloned.1.call-done = bf16[2,512,1,768]{3,1,2,0:T(8,128)(2,1)} async-done(((bf16[2,128,1,768]{3,1,2,0:T(8,128)(2,1)}), bf16[2,512,1,768]{3,1,2,0:T(8,128)(2,1)}) %all-gather.8.cloned.1.call-update) | async-done | bytes 1572880 | tf_op jit(solution)/shard_map/all_gather | solution.py:96
  31.5 3.0 %copy.333 = f32[2,512,1,768]{3,0,1,2:T(2,128)S(1)} copy(bf16[2,512,1,768]{3,1,2,0:T(8,128)(2,1)} %all-gather.8.cloned.1.call-done) | data formatting | bytes 4718592 | tf_op jit(solution)/shard_map/convert_element_type | solution.py:16
  47.9 1.4 convert_reduce_fusion
  49.3 1.3 fusion.69
  50.6 47.6 %all-gather.10.cloned.1.call-done = bf16[2,1024,1,768]{3,1,2,0:T(8,128)(2,1)} async-done(((bf16[2,128,1,768]{3,1,2,0:T(8,128)(2,1)}), bf16[2,1024,1,768]{3,1,2,0:T(8,128)(2,1)}) %all-gather.10.cloned.1.call-update) | async-done | bytes 3145744 | tf_op jit(solution)/shard_map/all_gather | solution.py:104
  98.2 5.1 %copy.349 = f32[2,1024,1,768]{3,0,1,2:T(2,128)S(1)} copy(bf16[2,1024,1,768]{3,1,2,0:T(8,128)(2,1)} %all-gather.10.cloned.1.call-done) | data formatting | bytes 9437184 | tf_op jit(solution)/shard_map/convert_element_type | solution.py:16
  103.3 2.3 %fusion.1 = bf16[2,512,1,768]{3,0,2,1:T(2,128)(2,1)S(1)} fusion(f32[2,512,2,768]{3,0,2,1:T(2,128)S(1)} %bitcast.262), kind=kLoop, calls=%fused_computation.2 | loop fusion | flops 2359296 | bytes 7864320 | tf_op jit(solution)/shard_map/convert_element_type | solution.py:19
  105.6 1.1 bitcast_convert_fusion
  112.6 1.4 copy.361
  114.0 2.2 %constant_dynamic-slice_fusion.1 = (bf16[1,128,1,768]{3,0,2,1:T(2,128)(2,1)}, bf16[1,128,1,768]{3,0,2,1:T(2,128)(2,1)}, bf16[1,128,1,768]{3,0,2,1:T(2,128)(2,1)}, bf16[1,128,1,768]{3,0,2,1:T(2,128)(2,1)S(1)}) fusion(bf16[2,512,1,768]{3,0,2,1:T(2,128)(2,1)S(1)} %fusion.1, s32[]{:T(128)S(6)} %select_n.18, s32[]{:T(128)S(6)} %add.230, ...), kind=kLoop, calls=%fused_computation.114 | loop fusion | bytes 1572876 | tf_op jit(solution)/shard_map/slice | solution.py:74
  116.2 1.2 copy.352
  117.4 1.2 copy.350
  118.6 1.1 fusion.65
  120.8 2.1 %constant_dynamic-slice_fusion = (bf16[1,128,1,768]{3,1,2,0:T(8,128)(2,1)S(1)}, bf16[1,128,1,768]{3,1,2,0:T(8,128)(2,1)S(1)}, bf16[1,128,1,768]{3,1,2,0:T(8,128)(2,1)}, bf16[1,128,1,768]{3,1,2,0:T(8,128)(2,1)}) fusion(bf16[2,1024,1,768]{3,1,2,0:T(8,128)(2,1)} %all-gather.10.cloned.1.call-done, s32[]{:T(128)S(6)} %select_n.17, s32[]{:T(128)S(6)} %add.230, ...), kind=kLoop, calls=%fused_computation.113 | loop fusion | bytes 1572876 | tf_op jit(solution)/shard_map/slice | solution.py:74
  124.8 1.1 copy.348
  128.8 1.7 copy.328
  130.5 1.7 copy.325
  132.3 1.4 fusion.68
  134.2 1.9 %fusion.31 = f32[12,64,128]{2,1,0:T(8,128)} fusion(bf16[128,12,64]{0,2,1:T(8,128)(2,1)} %bitcast.281, f32[12,128,128]{1,2,0:T(8,128)S(1)} %get-tuple-element.57, f32[12,128]{1,0:T(8,128)S(1)} %get-tuple-element.56), kind=kOutput, calls=%fused_computation.68 | convolution fusion | flops 25559040 | bytes 1382400 | tf_op jit(solution)/shard_map/ghqk,gkhe->gqhe/dot_general | solution.py:44
  136.1 1.9 %copy.330 = f32[128,768]{1,0:T(8,128)} copy(f32[128,768]{0,1:T(8,128)} %bitcast.271) | data formatting | bytes 786432 | tf_op jit(solution)/shard_map/reshape | solution.py:47
  138.0 2.2 %broadcast_in_dim.31 = f32[128,2,768]{2,1,0:T(2,128)} broadcast(f32[128,768]{1,0:T(8,128)} %copy.330), dimensions={0,2} | broadcast | bytes 1179648 | tf_op jit(solution)/shard_map/broadcast_in_dim | solution.py:53
  140.2 2.6 %reshape_reshape.22 = f32[256,768]{1,0:T(8,128)} reshape(f32[128,2,768]{2,1,0:T(2,128)} %broadcast_in_dim.31) | data formatting | bytes 1572864 | tf_op jit(solution)/shard_map/reshape;reshape | solution.py:66
  142.8 2.3 %copy.332 = f32[256,768]{0,1:T(8,128)} copy(f32[256,768]{1,0:T(8,128)} %reshape_reshape.22) | data formatting | bytes 1572864 | tf_op jit(solution)/shard_map/reshape;reshape | solution.py:66
  146.8 1.5 reshape.690
  150.1 1.6 reshape.688
  151.6 1.2 convert_reduce_fusion.4
  153.6 1.7 reshape.686
  155.2 1.6 convert_reduce_fusion.2
  158.4 1.4 convert_reduce_fusion.1
  165.5 1.9 %fusion.26 = bf16[256,768]{0,1:T(8,128)(2,1)S(1)} fusion(f32[256,768]{0,1:T(8,128)S(1)} %copy.361, f32[256,768]{0,1:T(8,128)S(1)} %copy.354, f32[256,768]{0,1:T(8,128)S(1)} %copy-done, f32[256,768]{0,1:T(8,128)S(1)} %copy.341, f32[256,768]{0,1:T(8,128)} %copy.332, f32[12,256,64]{1,2,0:T(8,128)} %fusion.69, f32[256,12]{0,1:T(8,128)S(1)} %get-tuple-element.5, ...), kind=kLoop, calls=%fused_computation.54 | loop fusion | flops 3342336 | bytes 5246976 | tf_op jit(solution)/shard_map/convert_element_type | solution.py:117
  167.5 2.5 %convolution_convert_fusion = bf16[256,768]{1,0:T(8,128)(2,1)} fusion(bf16[256,768]{0,1:T(8,128)(2,1)S(1)} %fusion.26, bf16[768,768]{1,0:T(8,128)(2,1)} %all-gather.6.cloned.1.call-done), kind=kOutput, calls=%fused_computation.13 | convolution fusion | flops 302186496 | bytes 1966080 | tf_op jit(solution)/shard_map/dot_general | solution.py:119
  (135 shorter events, 37.9 us)
Async XLA Ops:
  6.5 1.3 copy-start.3
  6.5 25.0 %all-gather.8.cloned.1.call-start = ((), (), s32[]{:S(2)}) async-start(), calls=%async_computation.1 | async-start | bytes 1966080 | tf_op jit(solution)/shard_map/all_gather | solution.py:96
  9.0 89.2 %all-gather.10.cloned.1.call-start = ((), (), s32[]{:S(2)}) async-start(), calls=%async_computation.2 | async-start | bytes 3538944 | tf_op jit(solution)/shard_map/all_gather | solution.py:104
  36.6 1.6 copy-start.5
  37.5 129.9 %all-gather.6.cloned.1.call-start = ((), (), s32[]{:S(2)}) async-start(), calls=%async_computation | async-start | bytes 1327104 | tf_op jit(solution)/shard_map/all_gather | solution.py:121
  38.7 1.7 copy-start.2
  39.4 1.5 copy-start.19
  110.7 0.6 copy-start.15
  110.7 1.9 %copy-start.8 = (f32[12,8,128]{2,1,0:T(8,128)}, f32[12,8,128]{2,1,0:T(8,128)S(1)}, u32[]{:S(2)}) copy-start(f32[12,8,128]{2,1,0:T(8,128)S(1)} %get-tuple-element.49) | copy-start | bytes 147460
  119.7 0.6 copy-start.6
  119.7 0.8 copy-start.13
  120.8 2.4 %copy-start.9 = (bf16[32,12,64]{2,1,0:T(8,128)(2,1)S(1)}, bf16[32,12,64]{2,1,0:T(8,128)(2,1)}, u32[]{:S(2)}) copy-start(bf16[32,12,64]{2,1,0:T(8,128)(2,1)} %convert_element_type.207) | copy-start | bytes 147460
  120.8 2.4 %copy-start.17 = (f32[12]{0:T(128)S(1)}, f32[12]{0:T(128)}, u32[]{:S(2)}) copy-start(f32[12]{0:T(128)} %get-tuple-element.45) | copy-start | bytes 148
  123.5 0.7 copy-start.1
  123.5 1.1 copy-start.12
  124.4 1.5 copy-start.4
  124.7 2.3 %copy-start.7 = (bf16[64,12,64]{2,1,0:T(8,128)(2,1)S(1)}, bf16[64,12,64]{2,1,0:T(8,128)(2,1)}, u32[]{:S(2)}) copy-start(bf16[64,12,64]{2,1,0:T(8,128)(2,1)} %convert_element_type.199) | copy-start | bytes 294916
  124.8 2.3 %copy-start.18 = (f32[12]{0:T(128)S(1)}, f32[12]{0:T(128)}, u32[]{:S(2)}) copy-start(f32[12]{0:T(128)} %get-tuple-element.44) | copy-start | bytes 148
  127.3 0.6 copy-start.11
  133.6 0.6 copy-start.10
  159.8 3.8 %copy-start.14 = (f32[12,16]{1,0:T(8,128)S(1)}, f32[12,16]{1,0:T(8,128)}, u32[]{:S(2)}) copy-start(f32[12,16]{1,0:T(8,128)} %copy-done.13) | copy-start | bytes 2308
  159.8 4.9 %copy-start.16 = (f32[256,12]{0,1:T(8,128)S(1)}, f32[256,12]{0,1:T(8,128)}, u32[]{:S(2)}) copy-start(f32[256,12]{0,1:T(8,128)} %copy.365) | copy-start | bytes 36868
  159.8 5.7 %copy-start = (f32[256,768]{0,1:T(8,128)S(1)}, f32[256,768]{0,1:T(8,128)}, u32[]{:S(2)}) copy-start(f32[256,768]{0,1:T(8,128)} %copy.348) | copy-start | bytes 2359300
Sparse Core Ops, SparseCore 0:
  9.1 22.3 all-gather.7
  37.6 60.4 all-gather.9
  100.3 39.6 all-gather.5
where the time goes:
time: 178 us; the launch traced here: 177 us
  waiting for transfers between devices  70.6 us (40%)
  local copies, waits for them, and re-layouts  59.7 us (34%)
  other arithmetic  20.6 us (12%)
  between operations  13.8 us (8%)
  matrix products  11.6 us (7%)
    all_gather x1, waiting for transfers between devices, on_device(): group_rows = lax.all_gather(group_rows, 'coarse', axis=1, tiled=True)  47.6 us
    all_gather x1, waiting for transfers between devices, on_device(): group_rows = lax.all_gather(own_pair, 'fine', axis=1, tiled=True)  22.5 us
    slice x8, local copies, waits for them, and re-layouts, far_level(): sibling[0][None]  8.98 us
    convert_element_type x7, local copies, waits for them, and re-layouts, coarsen(): row_data.reshape(dims_all[:-2] + (dims_all[-2] // 2, 2, dims_all[-1]))  8.92 us
    another operation x8, local copies, waits for them, and re-layouts, merge(): numer_b.reshape(row_count, head_count, -1) * scale_b[:, :, None]  8.27 us
    reduce_sum x6, other arithmetic, attend(): row_sum = jnp.sum(p_weights.astype(jnp.float32), axis=3)  7.63 us
    broadcast_in_dim x14, local copies, waits for them, and re-layouts, widen(): return tuple((jnp.repeat(member, factor, axis=0) for member in level_stat))  7.34 us
    convert_element_type x10, other arithmetic, coarsen(): return ((paired[..., 0, :] + paired[..., 1, :]) * 0.5).astype(jnp.bfloat16)  6.94 us
  transfers between devices with their start and end apart: 3, of which 2 were waited for; matrix products, arithmetic and copies ran while one was open for 44% of the time, Pallas kernels for 0%

commit v1 on v0

v1 whole, which is shorter than its diff:
```python
import functools
import math

import jax
import jax.numpy as jnp
from jax import lax
from jax.experimental import pallas as pl
from jax.experimental.pallas import tpu as pltpu
from jax.sharding import PartitionSpec as P

BLOCK = 128
LANES = 128
LOG_TWO = math.log(2.0)
NEG = -1e30
BF = jnp.bfloat16
F32 = jnp.float32
MESH = pl.DeviceIdType.MESH


def rows_at(tokens, level):
    return max(16, tokens >> level)


def dot(a, b):
    return jnp.dot(a, b, preferred_element_type=F32)


def grid_ids(rows, cols):
    return (
        lax.broadcasted_iota(jnp.int32, (rows, cols), 0),
        lax.broadcasted_iota(jnp.int32, (rows, cols), 1),
    )


def pair_mean(rows, cols):
    r, c = grid_ids(rows, cols)
    return jnp.where(c // 2 == r, 0.5, 0.0).astype(BF)


def repeat_matrix(rows, cols):
    r, c = grid_ids(rows, cols)
    return jnp.where(r // 2 == c, 1.0, 0.0).astype(BF)


def stacked_mean(which):
    r, c = grid_ids(16, 16)
    if which == "key":
        hit = (r < 8) & (c // 2 == r)
    elif which == "value":
        hit = (r >= 8) & (c // 2 == r - 8)
    else:
        hit = ((r < 8) & (c < 8) & (c // 2 == r)) | (
            (r >= 8) & (c >= 8) & ((c - 8) // 2 == r - 8)
        )
    return jnp.where(hit, 0.5, 0.0).astype(BF)


def loop(count, body):
    if count <= 8:
        for k in range(count):
            body(k)
    else:

        def step(k, carry):
            body(k)
            return carry

        lax.fori_loop(0, count, step, 0)


def wait_bytes(ref, sem):
    pltpu.make_async_copy(ref, ref, sem).wait()


def attend(q, k, v, gains, coarse_ref, valid):
    rows = q.shape[0]
    keys = k.shape[0]
    left = lax.broadcasted_iota(jnp.int32, (1, LANES), 1) < LANES // 2
    zero = jnp.zeros_like(q)
    q2 = jnp.concatenate([jnp.where(left, q, zero), jnp.where(left, zero, q)], axis=0)
    s = lax.dot_general(q2, k, (((1,), (1,)), ((), ())), preferred_element_type=F32)
    if valid < 8:
        key_no = lax.broadcasted_iota(jnp.int32, (1, keys), 1)
        s = jnp.where(key_no % 8 < valid, s, NEG)
    top = jnp.max(s, axis=1, keepdims=True)
    if coarse_ref:
        row_no = lax.broadcasted_iota(jnp.int32, (2 * rows, 1), 0)
        gain = jnp.where(row_no < rows, gains[0], gains[1])
        top = (top + gain).astype(BF).astype(F32)
        p = jnp.exp(s - (top - gain)).astype(BF)
    else:
        p = jnp.exp(s - top).astype(BF)
    v_ones = jnp.concatenate([v, jnp.ones((keys, LANES), BF)], axis=1)
    o = dot(p, v_ones)
    top = jnp.broadcast_to(top, (2 * rows, LANES))
    pick = lambda x: jnp.where(left, x[:rows], x[rows:])
    return pick(top), pick(o[:, LANES:]), pick(o[:, :LANES])


def kernel(fine_n, coarse_n, tokens, width, heads, *refs):
    n_dev = fine_n * coarse_n
    chips = n_dev // 2
    last = n_dev.bit_length() - 1
    pairs = width // LANES
    half_w = width // 2
    zs = coarse_n // 2
    it = iter(refs)
    q_ref, k_ref, v_ref, slope_ref, w_ref, out_ref = (next(it) for _ in range(6))
    q_lv = [None] + [next(it) for _ in range(last)]
    own = [None] + [next(it) for _ in range(last)]
    sib = [None] + [next(it) for _ in range(last)]
    state = [next(it) for _ in range(last + 1)]
    wbuf = next(it)
    att = next(it)
    send_sem, recv_sem, fsend_sem, frecv_sem, wsend_sem, wrecv_sem = (next(it) for _ in range(6))

    f = lax.axis_index("fine")
    c = lax.axis_index("coarse")
    dev = c * fine_n + f
    core = f % 2
    chip = dev // 2
    z = c // 2
    y = c % 2
    cols = pl.ds(pl.multiple_of(core * half_w, LANES), half_w)

    def at(chip_no):
        d = chip_no * 2 + core
        return {"fine": d % fine_n, "coarse": d // fine_n}

    other_core = {"fine": f + 1 - 2 * core, "coarse": c}
    flip_y = {"fine": f, "coarse": c + 1 - 2 * y}

    wbuf[z, y] = w_ref[...]

    barrier = pltpu.get_barrier_semaphore()
    pl.semaphore_signal(barrier, inc=1, device_id=other_core, device_id_type=MESH)

    def greet(k):
        pl.semaphore_signal(
            barrier, inc=1, device_id=at((chip + k + 1) % chips), device_id_type=MESH
        )

    loop(chips - 1, greet)

    for level in range(1, last + 1):
        rows, prev = rows_at(tokens, level), rows_at(tokens, level - 1)
        mean = pair_mean(rows, prev)
        if level == 1:
            q_prev, k_prev, v_prev = q_ref[...] * jnp.asarray(0.125, BF), k_ref[...], v_ref[...]
        q_prev = dot(mean, q_prev).astype(BF)
        q_lv[level][...] = q_prev
        if tokens >> level >= 16:
            k_prev = dot(mean, k_prev).astype(BF)
            v_prev = dot(mean, v_prev).astype(BF)
            own[level][0] = k_prev
            own[level][1] = v_prev
        else:
            if tokens >> level == 8:
                both = dot(stacked_mean("key"), k_prev) + dot(stacked_mean("value"), v_prev)
            else:
                both = dot(stacked_mean("both"), both)
            both = both.astype(BF)
            own[level][...] = both

    pl.semaphore_wait(barrier, chips)

    def remote(src, dst, s_sem, r_sem, dev_id):
        return pltpu.make_async_remote_copy(
            src_ref=src, dst_ref=dst, send_sem=s_sem, recv_sem=r_sem,
            device_id=dev_id, device_id_type=MESH,
        )

    def w_first(k):
        z_to = (z + k + 1) % zs
        remote(
            w_ref.at[:, cols], wbuf.at[z, y, :, cols], wsend_sem.at[0], wrecv_sem.at[0],
            {"fine": f, "coarse": z_to * 2 + y},
        ).start()

    def half_of(level, which):
        if tokens >> level >= 16:
            return sib[level].at[:, pl.ds(pl.multiple_of(which * 64, 16), 64), :]
        n = sib[level].shape[0] // 2
        return sib[level].at[pl.ds(pl.multiple_of(which * n, 16), n), :]

    def send_level(level):
        group = 2 ** (level - 2)
        rows = rows_at(tokens, level)
        mine = chip % group
        g = chip // group
        base = (g + 1 - 2 * (g % 2)) * group

        if tokens >> level >= 16:
            start = pl.multiple_of(core * 64 + mine * rows, 16)
            dst = sib[level].at[:, pl.ds(start, rows), :]
        else:
            start = pl.multiple_of((core * group + mine) * 16, 16)
            dst = sib[level].at[pl.ds(start, 16), :]

        def one(k):
            to = base + (mine + k) % group
            remote(own[level], dst, send_sem.at[level], recv_sem.at[level], at(to)).start()

        loop(group, one)

    first = remote(own[1], sib[1], send_sem.at[1], recv_sem.at[1], other_core)
    first.start()
    for level in range(2, last + 1):
        send_level(level)
    loop(zs - 1, w_first)

    gain_of = lambda level, h: level * LOG_TWO * (1.0 - slope_ref[h])

    def run_level(level):
        rows = rows_at(tokens, level)
        valid = tokens >> level
        for p in range(pairs):
            cs = slice(p * LANES, (p + 1) * LANES)
            if level == 0:
                q = q_ref[:, cs] * jnp.asarray(0.125, BF)
                k, v = k_ref[:, cs], v_ref[:, cs]
            else:
                q = q_lv[level][:, cs]
                if valid >= 16:
                    k, v = sib[level][0, :, cs], sib[level][1, :, cs]
                else:
                    n = sib[level].shape[0] // 16
                    both = sib[level][:, cs].astype(F32).reshape(n, 2, 8, LANES)
                    k = both[:, 0].reshape(n * 8, LANES).astype(BF)
                    v = both[:, 1].reshape(n * 8, LANES).astype(BF)
            gains = (gain_of(level, 2 * p), gain_of(level, 2 * p + 1))
            m, den, num = attend(q, k, v, gains, level > 0, valid)
            state[level][0, :, cs] = m
            state[level][1, :, cs] = den
            state[level][2, :, cs] = num

    def forward(level):
        half = half_of(level, core)
        wait_bytes(half, recv_sem.at[level])
        remote(half, half, fsend_sem.at[level], frecv_sem.at[level], other_core).start()

    run_level(0)
    forward(2)
    first.wait_recv()
    run_level(1)
    for level in range(3, last + 1):
        forward(level)
    wait_bytes(wbuf.at[pl.ds(0, zs - 1), 0, :, cols], wrecv_sem.at[0])
    to_y = remote(
        wbuf.at[:, y, :, cols], wbuf.at[:, y, :, cols], wsend_sem.at[1], wrecv_sem.at[1], flip_y
    )
    to_y.start()
    for level in range(2, last + 1):
        wait_bytes(half_of(level, 1 - core), frecv_sem.at[level])
        run_level(level)
    to_y.wait_recv()
    to_core = remote(
        wbuf.at[:, :, :, cols], wbuf.at[:, :, :, cols], wsend_sem.at[2], wrecv_sem.at[2], other_core
    )
    to_core.start()

    def widen(e, m, den, num):
        def split(x):
            hi = x.astype(BF)
            lo = (x - hi.astype(F32)).astype(BF)
            return dot(e, hi) + dot(e, lo)

        return dot(e, m.astype(BF)), split(den), split(num)

    def merge(a, b):
        top = jnp.maximum(a[0], b[0])
        sa, sb = jnp.exp(a[0] - top), jnp.exp(b[0] - top)
        return top, a[1] * sa + b[1] * sb, a[2] * sa + b[2] * sb

    for p in range(pairs):
        cs = slice(p * LANES, (p + 1) * LANES)
        now = tuple(state[last][i, :, cs] for i in range(3))
        for level in range(last - 1, -1, -1):
            e = repeat_matrix(rows_at(tokens, level), rows_at(tokens, level + 1))
            now = merge(widen(e, *now), tuple(state[level][i, :, cs] for i in range(3)))
        att[:, cs] = (now[2] / now[1]).astype(BF)

    to_core.wait_recv()
    if wbuf.shape[2] % 16 == 0:
        w_all = wbuf[...].reshape(width, width)
    else:
        w_all = wbuf[...].astype(F32).reshape(width, width).astype(BF)
    out_ref[...] = dot(att[...], w_all).astype(BF)

    first.wait_send()
    for level in range(2, last + 1):
        half = half_of(level, core)
        wait_bytes(half, send_sem.at[level])
        wait_bytes(half, fsend_sem.at[level])
    wait_bytes(wbuf.at[pl.ds(0, zs - 1), 0, :, cols], wsend_sem.at[0])
    to_y.wait_send()
    to_core.wait_send()


def on_device(fine_n, coarse_n, query_rows, key_rows, value_rows, distance_slope, out_weight):
    tokens, width = query_rows.shape
    heads = distance_slope.shape[0]
    last = (fine_n * coarse_n).bit_length() - 1
    levels = range(1, last + 1)
    q_lv = [pltpu.VMEM((rows_at(tokens, l), width), BF) for l in levels]
    own, sib = [], []
    for l in levels:
        if tokens >> l >= 16:
            own.append(pltpu.VMEM((2, tokens >> l, width), BF))
            sib.append(pltpu.VMEM((2, BLOCK, width), BF))
        else:
            own.append(pltpu.VMEM((16, width), BF))
            sib.append(pltpu.VMEM((16 * 2 ** (l - 1), width), BF))
    state = [pltpu.VMEM((3, rows_at(tokens, l), width), F32) for l in range(last + 1)]
    dma = pltpu.SemaphoreType.DMA
    vmem = pl.BlockSpec(memory_space=pltpu.VMEM)
    return pl.pallas_call(
        functools.partial(kernel, fine_n, coarse_n, tokens, width, heads),
        out_shape=jax.ShapeDtypeStruct((tokens, width), BF),
        in_specs=[vmem, vmem, vmem, pl.BlockSpec(memory_space=pltpu.SMEM), vmem],
        out_specs=vmem,
        scratch_shapes=q_lv + own + sib + state + [
            pltpu.VMEM((coarse_n // 2, 2) + out_weight.shape, BF),
            pltpu.VMEM((tokens, width), BF),
            dma((last + 1,)), dma((last + 1,)), dma((last + 1,)), dma((last + 1,)),
            dma((3,)), dma((3,)),
        ],
        compiler_params=pltpu.CompilerParams(
            collective_id=0, has_side_effects=True, vmem_limit_bytes=48 * 2**20
        ),
        name="hierarchical_attention",
    )(query_rows, key_rows, value_rows, distance_slope, out_weight)


def solution(mesh):
    fine_n, coarse_n = mesh.shape["fine"], mesh.shape["coarse"]
    return jax.shard_map(
        functools.partial(on_device, fine_n, coarse_n),
        mesh=mesh,
        in_specs=(
            P(("coarse", "fine"), None),
            P(("coarse", "fine"), None),
            P(("coarse", "fine"), None),
            P(),
            P("coarse", None),
        ),
        out_specs=P(("coarse", "fine"), None),
        check_vma=False,
    )
```

time: 178 us -> 38.5 us (0.22)
  waiting for transfers between devices: 70.6 us -> 0 us
  local copies, waits for them, and re-layouts: 59.7 us -> 5.3 us
  Pallas kernels: 0 us -> 32.9 us
  other arithmetic: 20.6 us -> 0 us
  between operations: 13.8 us -> 0.01 us
  matrix products: 11.6 us -> 0 us
    all_gather x3 -> x0, waiting for transfers between devices: 70.1 us -> none  [the longest x1 47.6 us: on_device(): group_rows = lax.all_gather(group_rows, 'coarse', axis=1, tiled=True)]
    pallas_call x0 -> x1, Pallas kernels: none -> 32.9 us  [on_device(): pl.pallas_call(functools.partial(kernel, fine_n, coarse_n, tokens, width,...]
    slice x16 -> x0, local copies, waits for them, and re-layouts: 15.1 us -> none  [the longest x8 8.98 us: far_level(): sibling[0][None]]
    convert_element_type x12 -> x0, local copies, waits for them, and re-layouts: 12.8 us -> none  [the longest x7 8.92 us: coarsen(): row_data.reshape(dims_all[:-2] + (dims_all[-2] // 2, 2, dims_all[-1]))]
    dot_general x13 -> x0, matrix products: 11.6 us -> none  [the longest x6 4.75 us: attend(): jnp.einsum('gqhe,gkhe->ghqk', q_heads, k_heads, preferred_element_type=jn...]
    reshape x19 -> x0, local copies, waits for them, and re-layouts: 11.5 us -> none  [the longest x10 5.96 us: widen(): return tuple((jnp.repeat(member, factor, axis=0) for member in level_stat))]
    convert_element_type x17 -> x0, other arithmetic: 11.5 us -> none  [the longest x10 6.94 us: coarsen(): return ((paired[..., 0, :] + paired[..., 1, :]) * 0.5).astype(jnp.bfloat16)]
    another operation x12 -> x0, local copies, waits for them, and re-layouts: 9.69 us -> none  [the longest x8 8.27 us: merge(): numer_b.reshape(row_count, head_count, -1) * scale_b[:, :, None]]
  transfers between devices with their start and end apart: 3 -> 0, of which waited for: 2 -> 0; matrix products, arithmetic and copies ran while one was open for 44% -> 0% of each run, Pallas kernels for 0% -> 0%
where the time goes in v1:
time: 38.5 us; the launch traced here: 38.2 us
  Pallas kernels  32.9 us (85%)
  local copies, waits for them, and re-layouts  5.3 us (14%)
    pallas_call x1, Pallas kernels, on_device(): pl.pallas_call(functools.partial(kernel, fine_n, coarse_n, tokens, width,...  32.9 us
    unnamed x11, local copies, waits for them, and re-layouts  5.3 us

profile of v1, /device:TPU:0, one launch (start us, length us, event | category | flops | bytes accessed | tf_op | source)
XLA Modules:
  0.0 38.2 jit_solution(9269767171488310782)
XLA Ops:
  0.0 0.0 copy-start
  0.0 1.0 %copy-done = bf16[256,768]{1,0:T(8,128)(2,1)S(1)} copy-done((bf16[256,768]{1,0:T(8,128)(2,1)S(1)}, bf16[256,768]{1,0:T(8,128)(2,1)}, u32[]{:S(2)}) %copy-start) | copy-done | bytes 393240
  1.0 0.0 copy-start.1
  1.0 1.0 %copy-done.1 = bf16[256,768]{1,0:T(8,128)(2,1)S(1)} copy-done((bf16[256,768]{1,0:T(8,128)(2,1)S(1)}, bf16[256,768]{1,0:T(8,128)(2,1)}, u32[]{:S(2)}) %copy-start.1) | copy-done | bytes 393240
  2.0 0.0 copy-start.2
  2.0 1.0 %copy-done.2 = bf16[256,768]{1,0:T(8,128)(2,1)S(1)} copy-done((bf16[256,768]{1,0:T(8,128)(2,1)S(1)}, bf16[256,768]{1,0:T(8,128)(2,1)}, u32[]{:S(2)}) %copy-start.2) | copy-done | bytes 393240
  3.0 0.0 copy-start.3
  3.0 0.9 %copy-done.3 = bf16[96,768]{1,0:T(8,128)(2,1)S(1)} copy-done((bf16[96,768]{1,0:T(8,128)(2,1)S(1)}, bf16[96,768]{1,0:T(8,128)(2,1)}, u32[]{:S(2)}) %copy-start.3) | copy-done | bytes 147480
  3.9 0.0 copy-start.4
  3.9 0.7 %copy-done.4 = f32[12]{0:T(128)S(1)} copy-done((f32[12]{0:T(128)S(1)}, f32[12]{0:T(128)}, u32[]{:S(2)}) %copy-start.4) | copy-done | bytes 72
  4.6 32.9 %hierarchical_attention.1 = bf16[256,768]{1,0:T(8,128)(2,1)S(1)} custom-call(bf16[256,768]{1,0:T(8,128)(2,1)S(1)} %copy-done, bf16[256,768]{1,0:T(8,128)(2,1)S(1)} %copy-done.1, bf16[256,768]{1,0:T(8,128)(2,1)S(1)} %copy-done.2, f32[12]{0:T(128)S(1)} %copy-done.4, bf16[96,768]{1,0:T(8,128)(2,1)S(1)} %copy-done.3), custom_call_target="tpu_custom_call" | custom-call | tf_op jit(solution)/shard_map/hierarchical_attention/pallas_call | solution.py:317
  37.5 0.7 %copy.7 = bf16[256,768]{1,0:T(8,128)(2,1)} copy(bf16[256,768]{1,0:T(8,128)(2,1)S(1)} %hierarchical_attention.1) | data formatting | bytes 786432
Async XLA Ops:
  0.0 1.0 %copy-start = (bf16[256,768]{1,0:T(8,128)(2,1)S(1)}, bf16[256,768]{1,0:T(8,128)(2,1)}, u32[]{:S(2)}) copy-start(bf16[256,768]{1,0:T(8,128)(2,1)} %refs_0_.1) | copy-start | bytes 1179652
  1.0 1.0 %copy-start.1 = (bf16[256,768]{1,0:T(8,128)(2,1)S(1)}, bf16[256,768]{1,0:T(8,128)(2,1)}, u32[]{:S(2)}) copy-start(bf16[256,768]{1,0:T(8,128)(2,1)} %refs_1_.1) | copy-start | bytes 1179652
  2.0 1.0 %copy-start.2 = (bf16[256,768]{1,0:T(8,128)(2,1)S(1)}, bf16[256,768]{1,0:T(8,128)(2,1)}, u32[]{:S(2)}) copy-start(bf16[256,768]{1,0:T(8,128)(2,1)} %refs_2_.1) | copy-start | bytes 1179652
  3.0 0.9 %copy-start.3 = (bf16[96,768]{1,0:T(8,128)(2,1)S(1)}, bf16[96,768]{1,0:T(8,128)(2,1)}, u32[]{:S(2)}) copy-start(bf16[96,768]{1,0:T(8,128)(2,1)} %refs_4_.1) | copy-start | bytes 442372
  3.9 0.7 %copy-start.4 = (f32[12]{0:T(128)S(1)}, f32[12]{0:T(128)}, u32[]{:S(2)}) copy-start(f32[12]{0:T(128)} %refs_3_.1) | copy-start | bytes 148

commit v2 on v1

--- a/solution.py
+++ b/solution.py
@@ -105,14 +105,16 @@
     half_w = width // 2
     zs = coarse_n // 2
     it = iter(refs)
-    q_ref, k_ref, v_ref, slope_ref, w_ref, out_ref = (next(it) for _ in range(6))
+    q_hbm, k_hbm, v_hbm, slope_hbm, w_ref, out_ref = (next(it) for _ in range(6))
+    q_ref, k_ref, v_ref, slope_ref = (next(it) for _ in range(4))
     q_lv = [None] + [next(it) for _ in range(last)]
     own = [None] + [next(it) for _ in range(last)]
     sib = [None] + [next(it) for _ in range(last)]
     state = [next(it) for _ in range(last + 1)]
     wbuf = next(it)
     att = next(it)
-    send_sem, recv_sem, fsend_sem, frecv_sem, wsend_sem, wrecv_sem = (next(it) for _ in range(6))
+    send_sem, recv_sem, fsend_sem, frecv_sem = (next(it) for _ in range(4))
+    load_sem, z_send, z_recv, y_send, y_recv, core_send, core_recv = (next(it) for _ in range(7))
 
     f = lax.axis_index("fine")
     c = lax.axis_index("coarse")
@@ -130,7 +132,20 @@
     other_core = {"fine": f + 1 - 2 * core, "coarse": c}
     flip_y = {"fine": f, "coarse": c + 1 - 2 * y}
 
-    wbuf[z, y] = w_ref[...]
+    loads = [
+        pltpu.make_async_copy(a, b, load_sem.at[i])
+        for i, (a, b) in enumerate(
+            (
+                (k_hbm, k_ref),
+                (v_hbm, v_ref),
+                (q_hbm, q_ref),
+                (w_ref.at[:, cols], wbuf.at[z, y, :, cols]),
+                (slope_hbm, slope_ref),
+            )
+        )
+    ]
+    for load in loads:
+        load.start()
 
     barrier = pltpu.get_barrier_semaphore()
     pl.semaphore_signal(barrier, inc=1, device_id=other_core, device_id_type=MESH)
@@ -141,6 +156,9 @@
         )
 
     loop(chips - 1, greet)
+
+    for load in loads:
+        load.wait()
 
     for level in range(1, last + 1):
         rows, prev = rows_at(tokens, level), rows_at(tokens, level - 1)
@@ -173,9 +191,18 @@
     def w_first(k):
         z_to = (z + k + 1) % zs
         remote(
-            w_ref.at[:, cols], wbuf.at[z, y, :, cols], wsend_sem.at[0], wrecv_sem.at[0],
+            wbuf.at[z, y, :, cols], wbuf.at[z, y, :, cols], z_send.at[k], z_recv.at[k],
             {"fine": f, "coarse": z_to * 2 + y},
         ).start()
+
+    def w_second(k, z_from):
+        part = wbuf.at[z_from, y, :, cols]
+        remote(part, part, y_send.at[k], y_recv.at[k], flip_y).start()
+
+    def w_pass(k):
+        z_from = (z - (k + 1) + zs) % zs
+        wait_bytes(wbuf.at[z_from, y, :, cols], z_recv.at[k])
+        w_second(k + 1, z_from)
 
     def half_of(level, which):
         if tokens >> level >= 16:
@@ -203,11 +230,12 @@
 
         loop(group, one)
 
+    w_second(0, z)
+    loop(zs - 1, w_first)
     first = remote(own[1], sib[1], send_sem.at[1], recv_sem.at[1], other_core)
     first.start()
     for level in range(2, last + 1):
         send_level(level)
-    loop(zs - 1, w_first)
 
     gain_of = lambda level, h: level * LOG_TWO * (1.0 - slope_ref[h])
 
@@ -239,25 +267,24 @@
         wait_bytes(half, recv_sem.at[level])
         remote(half, half, fsend_sem.at[level], frecv_sem.at[level], other_core).start()
 
+    def w_third(which):
+        part = wbuf.at[:, which, :, cols]
+        copy = remote(part, part, core_send.at[which], core_recv.at[which], other_core)
+        copy.start()
+
     run_level(0)
     forward(2)
     first.wait_recv()
     run_level(1)
+    loop(zs - 1, w_pass)
+    w_third(y)
     for level in range(3, last + 1):
         forward(level)
-    wait_bytes(wbuf.at[pl.ds(0, zs - 1), 0, :, cols], wrecv_sem.at[0])
-    to_y = remote(
-        wbuf.at[:, y, :, cols], wbuf.at[:, y, :, cols], wsend_sem.at[1], wrecv_sem.at[1], flip_y
-    )
-    to_y.start()
     for level in range(2, last + 1):
         wait_bytes(half_of(level, 1 - core), frecv_sem.at[level])
         run_level(level)
-    to_y.wait_recv()
-    to_core = remote(
-        wbuf.at[:, :, :, cols], wbuf.at[:, :, :, cols], wsend_sem.at[2], wrecv_sem.at[2], other_core
-    )
-    to_core.start()
+    loop(zs, lambda k: wait_bytes(wbuf.at[(z - k + zs) % zs, 1 - y, :, cols], y_recv.at[k]))
+    w_third(1 - y)
 
     def widen(e, m, den, num):
         def split(x):
@@ -280,7 +307,9 @@
             now = merge(widen(e, *now), tuple(state[level][i, :, cs] for i in range(3)))
         att[:, cs] = (now[2] / now[1]).astype(BF)
 
-    to_core.wait_recv()
+    other_cols = pl.ds(pl.multiple_of((1 - core) * half_w, LANES), half_w)
+    for i in range(2):
+        wait_bytes(wbuf.at[:, i, :, other_cols], core_recv.at[i])
     if wbuf.shape[2] % 16 == 0:
         w_all = wbuf[...].reshape(width, width)
     else:
@@ -292,9 +321,11 @@
         half = half_of(level, core)
         wait_bytes(half, send_sem.at[level])
         wait_bytes(half, fsend_sem.at[level])
-    wait_bytes(wbuf.at[pl.ds(0, zs - 1), 0, :, cols], wsend_sem.at[0])
-    to_y.wait_send()
-    to_core.wait_send()
+    part = wbuf.at[z, y, :, cols]
+    loop(zs - 1, lambda k: wait_bytes(part, z_send.at[k]))
+    loop(zs, lambda k: wait_bytes(part, y_send.at[k]))
+    for i in range(2):
+        wait_bytes(wbuf.at[:, i, :, cols], core_send.at[i])
 
 
 def on_device(fine_n, coarse_n, query_rows, key_rows, value_rows, distance_slope, out_weight):
@@ -313,20 +344,21 @@
             sib.append(pltpu.VMEM((16 * 2 ** (l - 1), width), BF))
     state = [pltpu.VMEM((3, rows_at(tokens, l), width), F32) for l in range(last + 1)]
     dma = pltpu.SemaphoreType.DMA
+    zs = coarse_n // 2
     vmem = pl.BlockSpec(memory_space=pltpu.VMEM)
     return pl.pallas_call(
         functools.partial(kernel, fine_n, coarse_n, tokens, width, heads),
         out_shape=jax.ShapeDtypeStruct((tokens, width), BF),
-        in_specs=[vmem, vmem, vmem, pl.BlockSpec(memory_space=pltpu.SMEM), vmem],
+        in_specs=[pl.BlockSpec(memory_space=pltpu.HBM)] * 5,
         out_specs=vmem,
-        scratch_shapes=q_lv + own + sib + state + [
+        scratch_shapes=[pltpu.VMEM((tokens, width), BF)] * 3 + [pltpu.SMEM((heads,), F32)] + q_lv + own + sib + state + [
             pltpu.VMEM((coarse_n // 2, 2) + out_weight.shape, BF),
             pltpu.VMEM((tokens, width), BF),
             dma((last + 1,)), dma((last + 1,)), dma((last + 1,)), dma((last + 1,)),
-            dma((3,)), dma((3,)),
+            dma((5,)), dma((zs,)), dma((zs,)), dma((zs,)), dma((zs,)), dma((2,)), dma((2,)),
         ],
         compiler_params=pltpu.CompilerParams(
-            collective_id=0, has_side_effects=True, vmem_limit_bytes=48 * 2**20
+            collective_id=0, has_side_effects=True, vmem_limit_bytes=62 * 2**20
         ),
         name="hierarchical_attention",
     )(query_rows, key_rows, value_rows, distance_slope, out_weight)

time: 38.5 us -> 35.8 us (0.930)
  local copies, waits for them, and re-layouts: 5.3 us -> 1.77 us
  Pallas kernels: 32.9 us -> 33.9 us
    unnamed x11 -> x1, local copies, waits for them, and re-layouts: 5.3 us -> 1.77 us
    pallas_call x1, Pallas kernels: 32.9 us -> 33.9 us  [on_device(): pl.pallas_call(functools.partial(kernel, fine_n, coarse_n, tokens, width,...]
where the time goes in v2:
time: 35.8 us; the launch traced here: 35.7 us
  Pallas kernels  33.9 us (95%)
  local copies, waits for them, and re-layouts  1.77 us (5%)
    pallas_call x1, Pallas kernels, on_device(): pl.pallas_call(functools.partial(kernel, fine_n, coarse_n, tokens, width,...  33.9 us
    unnamed x1, local copies, waits for them, and re-layouts  1.77 us

profile of v2, /device:TPU:0, one launch (start us, length us, event | category | flops | bytes accessed | tf_op | source)
XLA Modules:
  0.0 35.7 jit_solution(13553623816648664845)
XLA Ops:
  0.0 33.9 %hierarchical_attention.1 = bf16[256,768]{1,0:T(8,128)(2,1)} custom-call(bf16[256,768]{1,0:T(8,128)(2,1)} %refs_0_.1, bf16[256,768]{1,0:T(8,128)(2,1)} %refs_1_.1, bf16[256,768]{1,0:T(8,128)(2,1)} %refs_2_.1, f32[12]{0:T(128)} %refs_3_.1, bf16[96,768]{1,0:T(8,128)(2,1)} %refs_4_.1), custom_call_target="tpu_custom_call" | custom-call | tf_op jit(solution)/shard_map/hierarchical_attention/pallas_call | solution.py:349
  33.9 1.8 %copy.7 = bf16[256,768]{1,0:T(8,128)(2,1)} copy(bf16[256,768]{1,0:T(8,128)(2,1)} %hierarchical_attention.1) | data formatting | bytes 786432

commit v3 on v2

--- a/solution.py
+++ b/solution.py
@@ -99,7 +99,7 @@
 
 def kernel(fine_n, coarse_n, tokens, width, heads, *refs):
     n_dev = fine_n * coarse_n
-    chips = n_dev // 2
+    fine_bits = fine_n.bit_length() - 2
     last = n_dev.bit_length() - 1
     pairs = width // LANES
     half_w = width // 2
@@ -129,6 +129,9 @@
         d = chip_no * 2 + core
         return {"fine": d % fine_n, "coarse": d // fine_n}
 
+    def flip(bit):
+        return chip + (1 - 2 * (chip // 2**bit % 2)) * 2**bit
+
     other_core = {"fine": f + 1 - 2 * core, "coarse": c}
     flip_y = {"fine": f, "coarse": c + 1 - 2 * y}
 
@@ -150,12 +153,15 @@
     barrier = pltpu.get_barrier_semaphore()
     pl.semaphore_signal(barrier, inc=1, device_id=other_core, device_id_type=MESH)
 
+    pl.semaphore_signal(barrier, inc=1, device_id=flip_y, device_id_type=MESH)
+    for bit in range(fine_bits):
+        pl.semaphore_signal(barrier, inc=1, device_id=at(flip(bit)), device_id_type=MESH)
+
     def greet(k):
-        pl.semaphore_signal(
-            barrier, inc=1, device_id=at((chip + k + 1) % chips), device_id_type=MESH
-        )
-
-    loop(chips - 1, greet)
+        peer = {"fine": f, "coarse": (z + k + 1) % zs * 2 + y}
+        pl.semaphore_signal(barrier, inc=1, device_id=peer, device_id_type=MESH)
+
+    loop(zs - 1, greet)
 
     for load in loads:
         load.wait()
@@ -180,7 +186,7 @@
             both = both.astype(BF)
             own[level][...] = both
 
-    pl.semaphore_wait(barrier, chips)
+    pl.semaphore_wait(barrier, 1 + fine_bits + zs)
 
     def remote(src, dst, s_sem, r_sem, dev_id):
         return pltpu.make_async_remote_copy(
@@ -210,36 +216,48 @@
         n = sib[level].shape[0] // 2
         return sib[level].at[pl.ds(pl.multiple_of(which * n, 16), n), :]
 
-    def send_level(level):
+    def block_of(level, start, count):
         group = 2 ** (level - 2)
-        rows = rows_at(tokens, level)
+        if tokens >> level >= 16:
+            rows = tokens >> level
+            at_row = pl.multiple_of(core * 64 + start * rows, 16)
+            return sib[level].at[:, pl.ds(at_row, rows * count), :]
+        return sib[level].at[pl.ds(pl.multiple_of((core * group + start) * 16, 16), 16 * count), :]
+
+    def piece(level, step):
+        group = 2 ** (level - 2)
         mine = chip % group
-        g = chip // group
-        base = (g + 1 - 2 * (g % 2)) * group
-
-        if tokens >> level >= 16:
-            start = pl.multiple_of(core * 64 + mine * rows, 16)
-            dst = sib[level].at[:, pl.ds(start, rows), :]
-        else:
-            start = pl.multiple_of((core * group + mine) * 16, 16)
-            dst = sib[level].at[pl.ds(start, 16), :]
-
-        def one(k):
-            to = base + (mine + k) % group
-            remote(own[level], dst, send_sem.at[level], recv_sem.at[level], at(to)).start()
-
-        loop(group, one)
-
+        if step == 0:
+            here = block_of(level, mine, 1)
+            return own[level], here, level - 2, here
+        width_b = 2 ** (step - 1)
+        n = mine // width_b
+        here = block_of(level, n * width_b, width_b)
+        there = block_of(level, (n + 1 - 2 * (n % 2)) * width_b, width_b)
+        return here, here, step - 1, there
+
+    def exchange(step):
+        for level in range(max(2, step + 1), last + 1):
+            if step >= 1:
+                got = piece(level, step - 1)[3]
+                wait_bytes(got, recv_sem.at[level * last + step - 1])
+            if step <= level - 2:
+                src, dst, bit, _ = piece(level, step)
+                sem = level * last + step
+                remote(src, dst, send_sem.at[sem], recv_sem.at[sem], at(flip(bit))).start()
+            else:
+                half = half_of(level, core)
+                remote(half, half, fsend_sem.at[level], frecv_sem.at[level], other_core).start()
+
+    first = remote(own[1], sib[1], send_sem.at[1], recv_sem.at[1], other_core)
+    first.start()
+    exchange(0)
     w_second(0, z)
     loop(zs - 1, w_first)
-    first = remote(own[1], sib[1], send_sem.at[1], recv_sem.at[1], other_core)
-    first.start()
-    for level in range(2, last + 1):
-        send_level(level)
 
     gain_of = lambda level, h: level * LOG_TWO * (1.0 - slope_ref[h])
 
-    def run_level(level):
+    def run_level(level, between=None):
         rows = rows_at(tokens, level)
         valid = tokens >> level
         for p in range(pairs):
@@ -261,25 +279,25 @@
             state[level][0, :, cs] = m
             state[level][1, :, cs] = den
             state[level][2, :, cs] = num
-
-    def forward(level):
-        half = half_of(level, core)
-        wait_bytes(half, recv_sem.at[level])
-        remote(half, half, fsend_sem.at[level], frecv_sem.at[level], other_core).start()
+            if between is not None:
+                between(p)
 
     def w_third(which):
         part = wbuf.at[:, which, :, cols]
         copy = remote(part, part, core_send.at[which], core_recv.at[which], other_core)
         copy.start()
 
-    run_level(0)
-    forward(2)
+    def rounds(p):
+        if p % 2 == 1 and p // 2 + 1 < last:
+            exchange(p // 2 + 1)
+
+    run_level(0, rounds)
     first.wait_recv()
+    for step in range(pairs // 2 + 1, last):
+        exchange(step)
     run_level(1)
     loop(zs - 1, w_pass)
     w_third(y)
-    for level in range(3, last + 1):
-        forward(level)
     for level in range(2, last + 1):
         wait_bytes(half_of(level, 1 - core), frecv_sem.at[level])
         run_level(level)
@@ -319,7 +337,8 @@
     first.wait_send()
     for level in range(2, last + 1):
         half = half_of(level, core)
-        wait_bytes(half, send_sem.at[level])
+        for step in range(level - 1):
+            wait_bytes(piece(level, step)[0], send_sem.at[level * last + step])
         wait_bytes(half, fsend_sem.at[level])
     part = wbuf.at[z, y, :, cols]
     loop(zs - 1, lambda k: wait_bytes(part, z_send.at[k]))
@@ -354,7 +373,7 @@
         scratch_shapes=[pltpu.VMEM((tokens, width), BF)] * 3 + [pltpu.SMEM((heads,), F32)] + q_lv + own + sib + state + [
             pltpu.VMEM((coarse_n // 2, 2) + out_weight.shape, BF),
             pltpu.VMEM((tokens, width), BF),
-            dma((last + 1,)), dma((last + 1,)), dma((last + 1,)), dma((last + 1,)),
+            dma(((last + 1) * last,)), dma(((last + 1) * last,)), dma((last + 1,)), dma((last + 1,)),
             dma((5,)), dma((zs,)), dma((zs,)), dma((zs,)), dma((zs,)), dma((2,)), dma((2,)),
         ],
         compiler_params=pltpu.CompilerParams(

time: 35.8 us -> 37.3 us (1.042)
  Pallas kernels: 33.9 us -> 35.3 us
    pallas_call x1, Pallas kernels: 33.9 us -> 35.3 us  [on_device(): pl.pallas_call(functools.partial(kernel, fine_n, coarse_n, tokens, width,...]
where the time goes in v3:
time: 37.3 us; the launch traced here: 37.1 us
  Pallas kernels  35.3 us (95%)
  local copies, waits for them, and re-layouts  1.77 us (5%)
    pallas_call x1, Pallas kernels, on_device(): pl.pallas_call(functools.partial(kernel, fine_n, coarse_n, tokens, width,...  35.3 us
    unnamed x1, local copies, waits for them, and re-layouts  1.77 us

profile of v3, /device:TPU:0, one launch (start us, length us, event | category | flops | bytes accessed | tf_op | source)
XLA Modules:
  0.0 37.1 jit_solution(11744406971101986394)
XLA Ops:
  0.0 35.3 %hierarchical_attention.1 = bf16[256,768]{1,0:T(8,128)(2,1)} custom-call(bf16[256,768]{1,0:T(8,128)(2,1)} %refs_0_.1, bf16[256,768]{1,0:T(8,128)(2,1)} %refs_1_.1, bf16[256,768]{1,0:T(8,128)(2,1)} %refs_2_.1, f32[12]{0:T(128)} %refs_3_.1, bf16[96,768]{1,0:T(8,128)(2,1)} %refs_4_.1), custom_call_target="tpu_custom_call" | custom-call | tf_op jit(solution)/shard_map/hierarchical_attention/pallas_call | solution.py:368
  35.4 1.8 %copy.7 = bf16[256,768]{1,0:T(8,128)(2,1)} copy(bf16[256,768]{1,0:T(8,128)(2,1)} %hierarchical_attention.1) | data formatting | bytes 786432

commit v4 on v2

--- a/solution.py
+++ b/solution.py
@@ -72,26 +72,31 @@
     pltpu.make_async_copy(ref, ref, sem).wait()
 
 
-def attend(q, k, v, gains, coarse_ref, valid):
-    rows = q.shape[0]
-    keys = k.shape[0]
+def head_scores(q, k):
     left = lax.broadcasted_iota(jnp.int32, (1, LANES), 1) < LANES // 2
     zero = jnp.zeros_like(q)
     q2 = jnp.concatenate([jnp.where(left, q, zero), jnp.where(left, zero, q)], axis=0)
-    s = lax.dot_general(q2, k, (((1,), (1,)), ((), ())), preferred_element_type=F32)
+    return lax.dot_general(q2, k, (((1,), (1,)), ((), ())), preferred_element_type=F32)
+
+
+def head_weights(s, gains, coarse_ref, valid):
     if valid < 8:
-        key_no = lax.broadcasted_iota(jnp.int32, (1, keys), 1)
+        key_no = lax.broadcasted_iota(jnp.int32, (1, s.shape[1]), 1)
         s = jnp.where(key_no % 8 < valid, s, NEG)
     top = jnp.max(s, axis=1, keepdims=True)
-    if coarse_ref:
-        row_no = lax.broadcasted_iota(jnp.int32, (2 * rows, 1), 0)
-        gain = jnp.where(row_no < rows, gains[0], gains[1])
-        top = (top + gain).astype(BF).astype(F32)
-        p = jnp.exp(s - (top - gain)).astype(BF)
-    else:
-        p = jnp.exp(s - top).astype(BF)
-    v_ones = jnp.concatenate([v, jnp.ones((keys, LANES), BF)], axis=1)
-    o = dot(p, v_ones)
+    if not coarse_ref:
+        return top, jnp.exp(s - top).astype(BF)
+    rows = s.shape[0] // 2
+    row_no = lax.broadcasted_iota(jnp.int32, (2 * rows, 1), 0)
+    gain = jnp.where(row_no < rows, gains[0], gains[1])
+    top = (top + gain).astype(BF).astype(F32)
+    return top, jnp.exp(s - (top - gain)).astype(BF)
+
+
+def head_sums(top, p, v):
+    rows = p.shape[0] // 2
+    left = lax.broadcasted_iota(jnp.int32, (1, LANES), 1) < LANES // 2
+    o = dot(p, jnp.concatenate([v, jnp.ones(v.shape, BF)], axis=1))
     top = jnp.broadcast_to(top, (2 * rows, LANES))
     pick = lambda x: jnp.where(left, x[:rows], x[rows:])
     return pick(top), pick(o[:, LANES:]), pick(o[:, :LANES])
@@ -239,28 +244,35 @@
 
     gain_of = lambda level, h: level * LOG_TWO * (1.0 - slope_ref[h])
 
-    def run_level(level):
-        rows = rows_at(tokens, level)
-        valid = tokens >> level
-        for p in range(pairs):
+    def operands(level, p):
+        cs = slice(p * LANES, (p + 1) * LANES)
+        if level == 0:
+            return q_ref[:, cs] * jnp.asarray(0.125, BF), k_ref[:, cs], v_ref[:, cs]
+        q = q_lv[level][:, cs]
+        if tokens >> level >= 16:
+            return q, sib[level][0, :, cs], sib[level][1, :, cs]
+        n = sib[level].shape[0] // 16
+        both = sib[level][:, cs].astype(F32).reshape(n, 2, 8, LANES)
+        k = both[:, 0].reshape(n * 8, LANES).astype(BF)
+        return q, k, both[:, 1].reshape(n * 8, LANES).astype(BF)
+
+    def run_units(units):
+        qkv = [operands(level, p) for level, p in units]
+        scores = [head_scores(q, k) for q, k, _ in qkv]
+        weights = [
+            head_weights(
+                s, (gain_of(level, 2 * p), gain_of(level, 2 * p + 1)), level > 0, tokens >> level
+            )
+            for s, (level, p) in zip(scores, units)
+        ]
+        sums = [head_sums(top, pw, v) for (top, pw), (_, _, v) in zip(weights, qkv)]
+        for (level, p), parts in zip(units, sums):
             cs = slice(p * LANES, (p + 1) * LANES)
-            if level == 0:
-                q = q_ref[:, cs] * jnp.asarray(0.125, BF)
-                k, v = k_ref[:, cs], v_ref[:, cs]
-            else:
-                q = q_lv[level][:, cs]
-                if valid >= 16:
-                    k, v = sib[level][0, :, cs], sib[level][1, :, cs]
-                else:
-                    n = sib[level].shape[0] // 16
-                    both = sib[level][:, cs].astype(F32).reshape(n, 2, 8, LANES)
-                    k = both[:, 0].reshape(n * 8, LANES).astype(BF)
-                    v = both[:, 1].reshape(n * 8, LANES).astype(BF)
-            gains = (gain_of(level, 2 * p), gain_of(level, 2 * p + 1))
-            m, den, num = attend(q, k, v, gains, level > 0, valid)
-            state[level][0, :, cs] = m
-            state[level][1, :, cs] = den
-            state[level][2, :, cs] = num
+            for i in range(3):
+                state[level][i, :, cs] = parts[i]
+
+    def run_levels(*levels):
+        run_units([(level, p) for level in levels for p in range(pairs)])
 
     def forward(level):
         half = half_of(level, core)
@@ -272,25 +284,28 @@
         copy = remote(part, part, core_send.at[which], core_recv.at[which], other_core)
         copy.start()
 
-    run_level(0)
+    for p in range(0, pairs, 2):
+        run_units([(0, i) for i in range(p, min(p + 2, pairs))])
     forward(2)
     first.wait_recv()
-    run_level(1)
+    run_levels(1)
     loop(zs - 1, w_pass)
     w_third(y)
     for level in range(3, last + 1):
         forward(level)
     for level in range(2, last + 1):
         wait_bytes(half_of(level, 1 - core), frecv_sem.at[level])
-        run_level(level)
+    run_levels(*range(2, last + 1))
     loop(zs, lambda k: wait_bytes(wbuf.at[(z - k + zs) % zs, 1 - y, :, cols], y_recv.at[k]))
     w_third(1 - y)
 
     def widen(e, m, den, num):
+        e2 = jnp.concatenate([e, e], axis=1)
+
         def split(x):
             hi = x.astype(BF)
             lo = (x - hi.astype(F32)).astype(BF)
-            return dot(e, hi) + dot(e, lo)
+            return dot(e2, jnp.concatenate([hi, lo], axis=0))
 
         return dot(e, m.astype(BF)), split(den), split(num)
 
@@ -299,13 +314,16 @@
         sa, sb = jnp.exp(a[0] - top), jnp.exp(b[0] - top)
         return top, a[1] * sa + b[1] * sb, a[2] * sa + b[2] * sb
 
+    now = tuple(state[last][i] for i in range(3))
+    for level in range(last - 1, 0, -1):
+        e = repeat_matrix(rows_at(tokens, level), rows_at(tokens, level + 1))
+        now = merge(widen(e, *now), tuple(state[level][i] for i in range(3)))
+    e = repeat_matrix(tokens, rows_at(tokens, 1))
     for p in range(pairs):
         cs = slice(p * LANES, (p + 1) * LANES)
-        now = tuple(state[last][i, :, cs] for i in range(3))
-        for level in range(last - 1, -1, -1):
-            e = repeat_matrix(rows_at(tokens, level), rows_at(tokens, level + 1))
-            now = merge(widen(e, *now), tuple(state[level][i, :, cs] for i in range(3)))
-        att[:, cs] = (now[2] / now[1]).astype(BF)
+        full = widen(e, *(x[:, cs] for x in now))
+        full = merge(full, tuple(state[0][i, :, cs] for i in range(3)))
+        att[:, cs] = (full[2] / full[1]).astype(BF)
 
     other_cols = pl.ds(pl.multiple_of((1 - core) * half_w, LANES), half_w)
     for i in range(2):

time: 35.8 us -> 30.8 us (0.86)
  Pallas kernels: 33.9 us -> 28.9 us
    pallas_call x1, Pallas kernels: 33.9 us -> 28.9 us  [on_device(): pl.pallas_call(functools.partial(kernel, fine_n, coarse_n, tokens, width,...]
where the time goes in v4:
time: 30.8 us; the launch traced here: 30.6 us
  Pallas kernels  28.9 us (94%)
  local copies, waits for them, and re-layouts  1.77 us (6%)
    pallas_call x1, Pallas kernels, on_device(): pl.pallas_call(functools.partial(kernel, fine_n, coarse_n, tokens, width,...  28.9 us
    unnamed x1, local copies, waits for them, and re-layouts  1.77 us

profile of v4, /device:TPU:0, one launch (start us, length us, event | category | flops | bytes accessed | tf_op | source)
XLA Modules:
  0.0 30.6 jit_solution(12162596165353996114)
XLA Ops:
  0.0 28.9 %hierarchical_attention.1 = bf16[256,768]{1,0:T(8,128)(2,1)} custom-call(bf16[256,768]{1,0:T(8,128)(2,1)} %refs_0_.1, bf16[256,768]{1,0:T(8,128)(2,1)} %refs_1_.1, bf16[256,768]{1,0:T(8,128)(2,1)} %refs_2_.1, f32[12]{0:T(128)} %refs_3_.1, bf16[96,768]{1,0:T(8,128)(2,1)} %refs_4_.1), custom_call_target="tpu_custom_call" | custom-call | tf_op jit(solution)/shard_map/hierarchical_attention/pallas_call | solution.py:367
  28.9 1.8 %copy.7 = bf16[256,768]{1,0:T(8,128)(2,1)} copy(bf16[256,768]{1,0:T(8,128)(2,1)} %hierarchical_attention.1) | data formatting | bytes 786432

commit v5 on v4

--- a/solution.py
+++ b/solution.py
@@ -104,7 +104,7 @@
 
 def kernel(fine_n, coarse_n, tokens, width, heads, *refs):
     n_dev = fine_n * coarse_n
-    chips = n_dev // 2
+    fine_bits = fine_n.bit_length() - 2
     last = n_dev.bit_length() - 1
     pairs = width // LANES
     half_w = width // 2
@@ -134,6 +134,9 @@
         d = chip_no * 2 + core
         return {"fine": d % fine_n, "coarse": d // fine_n}
 
+    def flip(bit):
+        return chip + (1 - 2 * (chip // 2**bit % 2)) * 2**bit
+
     other_core = {"fine": f + 1 - 2 * core, "coarse": c}
     flip_y = {"fine": f, "coarse": c + 1 - 2 * y}
 
@@ -155,12 +158,15 @@
     barrier = pltpu.get_barrier_semaphore()
     pl.semaphore_signal(barrier, inc=1, device_id=other_core, device_id_type=MESH)
 
+    pl.semaphore_signal(barrier, inc=1, device_id=flip_y, device_id_type=MESH)
+    for bit in range(fine_bits):
+        pl.semaphore_signal(barrier, inc=1, device_id=at(flip(bit)), device_id_type=MESH)
+
     def greet(k):
-        pl.semaphore_signal(
-            barrier, inc=1, device_id=at((chip + k + 1) % chips), device_id_type=MESH
-        )
-
-    loop(chips - 1, greet)
+        peer = {"fine": f, "coarse": (z + k + 1) % zs * 2 + y}
+        pl.semaphore_signal(barrier, inc=1, device_id=peer, device_id_type=MESH)
+
+    loop(zs - 1, greet)
 
     for load in loads:
         load.wait()
@@ -185,7 +191,7 @@
             both = both.astype(BF)
             own[level][...] = both
 
-    pl.semaphore_wait(barrier, chips)
+    pl.semaphore_wait(barrier, 1 + fine_bits + zs)
 
     def remote(src, dst, s_sem, r_sem, dev_id):
         return pltpu.make_async_remote_copy(
@@ -215,32 +221,44 @@
         n = sib[level].shape[0] // 2
         return sib[level].at[pl.ds(pl.multiple_of(which * n, 16), n), :]
 
-    def send_level(level):
+    def block_of(level, start, count):
         group = 2 ** (level - 2)
-        rows = rows_at(tokens, level)
+        if tokens >> level >= 16:
+            rows = tokens >> level
+            at_row = pl.multiple_of(core * 64 + start * rows, 16)
+            return sib[level].at[:, pl.ds(at_row, rows * count), :]
+        return sib[level].at[pl.ds(pl.multiple_of((core * group + start) * 16, 16), 16 * count), :]
+
+    def piece(level, step):
+        group = 2 ** (level - 2)
         mine = chip % group
-        g = chip // group
-        base = (g + 1 - 2 * (g % 2)) * group
-
-        if tokens >> level >= 16:
-            start = pl.multiple_of(core * 64 + mine * rows, 16)
-            dst = sib[level].at[:, pl.ds(start, rows), :]
-        else:
-            start = pl.multiple_of((core * group + mine) * 16, 16)
-            dst = sib[level].at[pl.ds(start, 16), :]
-
-        def one(k):
-            to = base + (mine + k) % group
-            remote(own[level], dst, send_sem.at[level], recv_sem.at[level], at(to)).start()
-
-        loop(group, one)
-
+        if step == 0:
+            here = block_of(level, mine, 1)
+            return own[level], here, level - 2, here
+        width_b = 2 ** (step - 1)
+        n = mine // width_b
+        here = block_of(level, n * width_b, width_b)
+        there = block_of(level, (n + 1 - 2 * (n % 2)) * width_b, width_b)
+        return here, here, step - 1, there
+
+    def exchange(step):
+        for level in range(max(2, step + 1), last + 1):
+            if step >= 1:
+                got = piece(level, step - 1)[3]
+                wait_bytes(got, recv_sem.at[level * last + step - 1])
+            if step <= level - 2:
+                src, dst, bit, _ = piece(level, step)
+                sem = level * last + step
+                remote(src, dst, send_sem.at[sem], recv_sem.at[sem], at(flip(bit))).start()
+            else:
+                half = half_of(level, core)
+                remote(half, half, fsend_sem.at[level], frecv_sem.at[level], other_core).start()
+
+    first = remote(own[1], sib[1], send_sem.at[1], recv_sem.at[1], other_core)
+    first.start()
+    exchange(0)
     w_second(0, z)
     loop(zs - 1, w_first)
-    first = remote(own[1], sib[1], send_sem.at[1], recv_sem.at[1], other_core)
-    first.start()
-    for level in range(2, last + 1):
-        send_level(level)
 
     gain_of = lambda level, h: level * LOG_TWO * (1.0 - slope_ref[h])
 
@@ -274,11 +292,6 @@
     def run_levels(*levels):
         run_units([(level, p) for level in levels for p in range(pairs)])
 
-    def forward(level):
-        half = half_of(level, core)
-        wait_bytes(half, recv_sem.at[level])
-        remote(half, half, fsend_sem.at[level], frecv_sem.at[level], other_core).start()
-
     def w_third(which):
         part = wbuf.at[:, which, :, cols]
         copy = remote(part, part, core_send.at[which], core_recv.at[which], other_core)
@@ -286,13 +299,14 @@
 
     for p in range(0, pairs, 2):
         run_units([(0, i) for i in range(p, min(p + 2, pairs))])
-    forward(2)
+        if p // 2 + 1 < last:
+            exchange(p // 2 + 1)
     first.wait_recv()
+    for step in range((pairs + 1) // 2 + 1, last):
+        exchange(step)
     run_levels(1)
     loop(zs - 1, w_pass)
     w_third(y)
-    for level in range(3, last + 1):
-        forward(level)
     for level in range(2, last + 1):
         wait_bytes(half_of(level, 1 - core), frecv_sem.at[level])
     run_levels(*range(2, last + 1))
@@ -337,7 +351,8 @@
     first.wait_send()
     for level in range(2, last + 1):
         half = half_of(level, core)
-        wait_bytes(half, send_sem.at[level])
+        for step in range(level - 1):
+            wait_bytes(piece(level, step)[0], send_sem.at[level * last + step])
         wait_bytes(half, fsend_sem.at[level])
     part = wbuf.at[z, y, :, cols]
     loop(zs - 1, lambda k: wait_bytes(part, z_send.at[k]))
@@ -372,7 +387,7 @@
         scratch_shapes=[pltpu.VMEM((tokens, width), BF)] * 3 + [pltpu.SMEM((heads,), F32)] + q_lv + own + sib + state + [
             pltpu.VMEM((coarse_n // 2, 2) + out_weight.shape, BF),
             pltpu.VMEM((tokens, width), BF),
-            dma((last + 1,)), dma((last + 1,)), dma((last + 1,)), dma((last + 1,)),
+            dma(((last + 1) * last,)), dma(((last + 1) * last,)), dma((last + 1,)), dma((last + 1,)),
             dma((5,)), dma((zs,)), dma((zs,)), dma((zs,)), dma((zs,)), dma((2,)), dma((2,)),
         ],
         compiler_params=pltpu.CompilerParams(

time: 30.8 us -> 33.9 us (1.10)
  the two profiles are of different devices: /device:TPU:0 before, /device:TPU:1 now
where the time goes in v5:
time: 33.9 us; the launch traced here: 33.8 us
  Pallas kernels  32 us (94%)
  local copies, waits for them, and re-layouts  1.77 us (5%)
    pallas_call x1, Pallas kernels, on_device(): pl.pallas_call(functools.partial(kernel, fine_n, coarse_n, tokens, width,...  32 us
    unnamed x1, local copies, waits for them, and re-layouts  1.77 us

profile of v5, /device:TPU:1, one launch (start us, length us, event | category | flops | bytes accessed | tf_op | source)
XLA Modules:
  0.0 33.8 jit_solution(14117034012005051653)
XLA Ops:
  0.0 32.0 %hierarchical_attention.1 = bf16[256,768]{1,0:T(8,128)(2,1)} custom-call(bf16[256,768]{1,0:T(8,128)(2,1)} %refs_0_.1, bf16[256,768]{1,0:T(8,128)(2,1)} %refs_1_.1, bf16[256,768]{1,0:T(8,128)(2,1)} %refs_2_.1, f32[12]{0:T(128)} %refs_3_.1, bf16[96,768]{1,0:T(8,128)(2,1)} %refs_4_.1), custom_call_target="tpu_custom_call" | custom-call | tf_op jit(solution)/shard_map/hierarchical_attention/pallas_call | solution.py:382
  32.0 1.8 %copy.7 = bf16[256,768]{1,0:T(8,128)(2,1)} copy(bf16[256,768]{1,0:T(8,128)(2,1)} %hierarchical_attention.1) | data formatting | bytes 786432
